TPU v7x, 32 devices: a whole 2x2x4 slice. The times are simulated.
32 devices in a mesh: dp: 4 (over y, x), seq: 8 (over z, core).
Axes of the slice: x: 2, y: 2, z: 4, core: 2. Of those that a mesh axis runs over, the one named last changes fastest.
Arguments:
- queries: bfloat16 [4096, 1152], P(('dp', 'seq')), may hold values from -6 to 6
- keys: bfloat16 [4096, 1152], P(('dp', 'seq')), may hold values from -6 to 6
- values: bfloat16 [4096, 1152], P(('dp', 'seq')), may hold values from -6 to 6
- out_grad: bfloat16 [4096, 1152], P(('dp', 'seq')), may hold values from -6 to 6
- out_weight: bfloat16 [1152, 1152], replicated, may hold values from -0.1875 to 0.1875
- extents: int32 [4, 8], P('dp'), may hold values from 1 to 8, 16 in all within a row
Outputs:
- query_grad: bfloat16 [4096, 1152], P(('dp', 'seq'))
- key_grad: bfloat16 [4096, 1152], P(('dp', 'seq'))
- value_grad: bfloat16 [4096, 1152], P(('dp', 'seq'))
- weight_grad: float32 [1152, 1152], P('seq', 'dp')
Inputs may be any that keep to these rules, and one draw needn't show every extreme that they name: `extents`: row i lists the 8 images packed in order into sequence i, in units of 64 tokens; each row sums to 16.
All inputs are finite; a program needn't handle non-finite values.
Results may differ from a plain program's by a relative error of at most 0.034.
Values may be sent and summed in bfloat16 or wider, within the bound.
A program may use at most 128 MiB of HBM per device.

v0:
```python
import math

import jax
import jax.numpy as jnp
from jax import lax
from jax.sharding import PartitionSpec as P

HEADS = 16
HEAD = 72
UNIT = 64


def local(queries, keys, values, out_grad, out_weight, extents):
    local_rows = queries.shape[0]
    model_width = queries.shape[1]
    seq_parts = lax.axis_size("seq")
    seq_length = local_rows * seq_parts
    block_len = math.gcd(seq_length, 512)
    num_blocks = seq_length // block_len
    score_scale = HEAD ** (-0.5)
    position = jnp.arange(seq_length, dtype=jnp.int32)
    image_ends = jnp.cumsum(extents[0]) * UNIT
    segment_all = jnp.sum((position[:, None] >= image_ends[None, :]).astype(jnp.int32), axis=1)
    segment_mine = lax.dynamic_slice_in_dim(
        segment_all, lax.axis_index("seq") * local_rows, local_rows
    )
    out_back = lax.dot_general(
        out_grad, out_weight, (((1,), (1,)), ((), ())), preferred_element_type=jnp.float32
    ).astype(jnp.bfloat16)
    key_all, value_all = (
        lax.all_gather(keys, "seq", axis=0, tiled=True),
        lax.all_gather(values, "seq", axis=0, tiled=True),
    )
    query_heads = queries.reshape(local_rows, HEADS, HEAD)
    key_heads = keys.reshape(local_rows, HEADS, HEAD)
    value_heads = values.reshape(local_rows, HEADS, HEAD)
    back_heads = out_back.reshape(local_rows, HEADS, HEAD)
    key_blocks = key_all.reshape(num_blocks, block_len, HEADS, HEAD)
    value_blocks = value_all.reshape(num_blocks, block_len, HEADS, HEAD)
    segment_blocks = segment_all.reshape(num_blocks, block_len)

    def mask_for(seg_block):
        return (segment_mine[:, None] == seg_block[None, :])[None]

    def query_scores(key_block):
        return (
            jnp.einsum("qhd,khd->hqk", query_heads, key_block, preferred_element_type=jnp.float32)
            * score_scale
        )

    def grow_total(carry, inputs):
        top_now, total_now = carry
        key_block, seg_block = inputs
        scores = query_scores(key_block)
        inside = mask_for(seg_block)
        top_next = jnp.maximum(top_now, jnp.max(jnp.where(inside, scores, -1e30), axis=2))
        total_next = total_now * jnp.exp(top_now - top_next) + jnp.sum(
            jnp.where(inside, jnp.exp(scores - top_next[:, :, None]), 0.0), axis=2
        )
        return ((top_next, total_next), None)

    start_top = jnp.full((HEADS, local_rows), -1e30, jnp.float32)
    start_total = jnp.zeros((HEADS, local_rows), jnp.float32)
    (top_all, total_all), unused = lax.scan(
        grow_total, (start_top, start_total), (key_blocks, segment_blocks)
    )
    log_total = top_all + jnp.log(total_all)

    def attend_block(carry, inputs):
        key_block, value_block, seg_block = inputs
        scores = query_scores(key_block)
        probs_low = jnp.where(
            mask_for(seg_block), jnp.exp(scores - log_total[:, :, None]), 0.0
        ).astype(jnp.bfloat16)
        return (
            carry
            + jnp.einsum(
                "hqk,khd->qhd", probs_low, value_block, preferred_element_type=jnp.float32
            ),
            None,
        )

    summed, unused = lax.scan(
        attend_block,
        jnp.zeros((local_rows, HEADS, HEAD), jnp.float32),
        (key_blocks, value_blocks, segment_blocks),
    )
    attended = summed.astype(jnp.bfloat16).reshape(local_rows, model_width)
    delta_rows = jnp.sum(
        (out_back.astype(jnp.float32) * attended.astype(jnp.float32)).reshape(
            local_rows, HEADS, HEAD
        ),
        axis=2,
    )
    lse_all, delta_all = (
        lax.all_gather(log_total.T, "seq", axis=0, tiled=True),
        lax.all_gather(delta_rows, "seq", axis=0, tiled=True),
    )
    query_all, back_all = (
        lax.all_gather(queries, "seq", axis=0, tiled=True),
        lax.all_gather(out_back, "seq", axis=0, tiled=True),
    )

    def query_side(carry, inputs):
        key_block, value_block, seg_block = inputs
        scores = query_scores(key_block)
        probs = jnp.where(mask_for(seg_block), jnp.exp(scores - log_total[:, :, None]), 0.0)
        dprobs = jnp.einsum(
            "qhd,khd->hqk", back_heads, value_block, preferred_element_type=jnp.float32
        )
        dscores = (probs * (dprobs - delta_rows.T[:, :, None])).astype(jnp.bfloat16)
        return (
            carry
            + jnp.einsum("hqk,khd->qhd", dscores, key_block, preferred_element_type=jnp.float32),
            None,
        )

    query_acc, unused = lax.scan(
        query_side,
        jnp.zeros((local_rows, HEADS, HEAD), jnp.float32),
        (key_blocks, value_blocks, segment_blocks),
    )
    query_grad = (query_acc * score_scale).astype(jnp.bfloat16).reshape(local_rows, model_width)
    query_blocks = query_all.reshape(num_blocks, block_len, HEADS, HEAD)
    back_blocks = back_all.reshape(num_blocks, block_len, HEADS, HEAD)
    lse_blocks = lse_all.reshape(num_blocks, block_len, HEADS)
    delta_blocks = delta_all.reshape(num_blocks, block_len, HEADS)

    def key_side(carry, inputs):
        key_acc, value_acc = carry
        query_block, back_block, lse_block, delta_block, seg_block = inputs
        scores = (
            jnp.einsum("khd,qhd->hkq", key_heads, query_block, preferred_element_type=jnp.float32)
            * score_scale
        )
        probs = jnp.where(mask_for(seg_block), jnp.exp(scores - lse_block.T[:, None, :]), 0.0)
        probs_low = probs.astype(jnp.bfloat16)
        value_acc = value_acc + jnp.einsum(
            "hkq,qhd->khd", probs_low, back_block, preferred_element_type=jnp.float32
        )
        dprobs = jnp.einsum(
            "khd,qhd->hkq", value_heads, back_block, preferred_element_type=jnp.float32
        )
        dscores = (probs * (dprobs - delta_block.T[:, None, :])).astype(jnp.bfloat16)
        key_acc = key_acc + jnp.einsum(
            "hkq,qhd->khd", dscores, query_block, preferred_element_type=jnp.float32
        )
        return ((key_acc, value_acc), None)

    start_acc = jnp.zeros((local_rows, HEADS, HEAD), jnp.float32)
    (key_acc, value_acc), unused = lax.scan(
        key_side,
        (start_acc, start_acc),
        (query_blocks, back_blocks, lse_blocks, delta_blocks, segment_blocks),
    )
    key_grad = (key_acc * score_scale).astype(jnp.bfloat16).reshape(local_rows, model_width)
    value_grad = value_acc.astype(jnp.bfloat16).reshape(local_rows, model_width)
    weight_term = lax.dot_general(
        attended, out_grad, (((0,), (0,)), ((), ())), preferred_element_type=jnp.float32
    )
    partial_sum = lax.psum_scatter(
        weight_term.astype(jnp.bfloat16), "seq", scatter_dimension=0, tiled=True
    )
    weight_grad = lax.psum_scatter(partial_sum, "dp", scatter_dimension=1, tiled=True).astype(
        jnp.float32
    )
    return (query_grad, key_grad, value_grad, weight_grad)


def solution(mesh):
    return jax.shard_map(
        local,
        mesh=mesh,
        in_specs=(
            P(("dp", "seq"), None),
            P(("dp", "seq"), None),
            P(("dp", "seq"), None),
            P(("dp", "seq"), None),
            P(),
            P("dp", None),
        ),
        out_specs=(
            P(("dp", "seq"), None),
            P(("dp", "seq"), None),
            P(("dp", "seq"), None),
            P("seq", "dp"),
        ),
        check_vma=False,
    )
```

profile of v0, /device:TPU:0, one launch (start us, length us, event | category | flops | bytes accessed | tf_op | source)
XLA Modules:
  0.0 262.1 jit_solution(13382776449502908337)
XLA Ops:
  11.7 32.3 %all-gather.5.cloned.1.call-done = bf16[1024,1152]{1,0:T(8,128)(2,1)} async-done(((bf16[128,1152]{1,0:T(8,128)(2,1)}), bf16[1024,1152]{1,0:T(8,128)(2,1)}) %all-gather.5.cloned.1.call-update) | async-done | bytes 2359312 | tf_op jit(solution)/shard_map/all_gather | solution.py:31
  44.0 9.6 %reshape.222 = bf16[2,512,16,72]{3,2,1,0:T(8,128)(2,1)} reshape(bf16[1024,1152]{1,0:T(8,128)(2,1)} %all-gather.5.cloned.1.call-done) | data formatting | bytes 4718592 | tf_op jit(solution)/shard_map/reshape | solution.py:38
  53.6 7.2 %copy.88 = bf16[2,512,16,72]{1,3,2,0:T(8,128)(2,1)} copy(bf16[2,512,16,72]{3,2,1,0:T(8,128)(2,1)} %reshape.222) | data formatting | bytes 4718592
  60.8 15.7 %all-gather.7.cloned.1.call-done = bf16[1024,1152]{1,0:T(8,128)(2,1)} async-done(((bf16[128,1152]{1,0:T(8,128)(2,1)}), bf16[1024,1152]{1,0:T(8,128)(2,1)}) %all-gather.7.cloned.1.call-update) | async-done | bytes 2359312 | tf_op jit(solution)/shard_map/all_gather | solution.py:32
  76.4 9.6 %reshape.223 = bf16[2,512,16,72]{3,2,1,0:T(8,128)(2,1)} reshape(bf16[1024,1152]{1,0:T(8,128)(2,1)} %all-gather.7.cloned.1.call-done) | data formatting | bytes 4718592 | tf_op jit(solution)/shard_map/reshape | solution.py:39
  86.0 7.1 %copy.89 = bf16[2,512,16,72]{1,3,2,0:T(8,128)(2,1)} copy(bf16[2,512,16,72]{3,2,1,0:T(8,128)(2,1)} %reshape.223) | data formatting | bytes 4718592
  93.1 15.0 %while.48 = (s32[]{:T(128)}, f32[16,128]{1,0:T(8,128)S(1)}, f32[16,128]{1,0:T(8,128)S(1)}, s32[128]{0:T(128)S(1)}, s32[2,512]{1,0:T(2,128)S(1)}, /*index=5*/bf16...) while((s32[]{:T(128)}, f32[16,128]{1,0:T(8,128)S(1)}, ...), condition=%wide.region_5.6_spmd.clone, body=%wide.region_2.5_spmd.clone.sunk | while | flops 158410752 | bytes 10173048 | solution.py:64
  93.3 4.2 %fusion.113 = (f32[16,128]{1,0:T(8,128)S(1)}, f32[16,512,128]{2,1,0:T(8,128)}) fusion(pred[128,512]{0,1:T(8,128)(4,1)S(1)} %broadcast_compare_fusion.8, bf16[128,16,72]{0,2,1:T(8,128)(2,1)S(1)} %get-tuple-element.796, bf16[2,512,16,72]{1,3,2,0:T(8,128)(2,1)} %get-tuple-element.795, s32[]{:T(128)S(6)} %copy.128), kind=kOutput, calls=%fused_computation.2.clone.1 | convolution fusion | flops 154138624 | bytes 5742596 | tf_op jit(solution)/shard_map/while/body/eval_jaxpr/qhd,khd->hqk/dot_general | solution.py:47
  100.8 4.2 %fusion.113 = (f32[16,128]{1,0:T(8,128)S(1)}, f32[16,512,128]{2,1,0:T(8,128)}) fusion(pred[128,512]{0,1:T(8,128)(4,1)S(1)} %broadcast_compare_fusion.8, bf16[128,16,72]{0,2,1:T(8,128)(2,1)S(1)} %get-tuple-element.796, bf16[2,512,16,72]{1,3,2,0:T(8,128)(2,1)} %get-tuple-element.795, s32[]{:T(128)S(6)} %copy.128), kind=kOutput, calls=%fused_computation.2.clone.1 | convolution fusion | flops 154138624 | bytes 5742596 | tf_op jit(solution)/shard_map/while/body/eval_jaxpr/qhd,khd->hqk/dot_general | solution.py:47
  108.1 8.4 %while.49 = (s32[]{:T(128)}, f32[128,16,72]{0,2,1:T(8,128)}, bf16[2,512,16,72]{1,3,2,0:T(8,128)(2,1)}, s32[128]{0:T(128)S(1)}, s32[2,512]{1,0:T(2,128)S(1)}, /*i...) while((s32[]{:T(128)}, f32[128,16,72]{0,2,1:T(8,128)}, ...), condition=%wide.region_7.8_spmd.clone, body=%wide.region_6.7_spmd.clone.sunk | while | flops 306544640 | bytes 3981434 | solution.py:83
  132.2 20.1 %while.50 = (s32[]{:T(128)}, f32[128,16,72]{0,2,1:T(8,128)}, bf16[2,512,16,72]{1,3,2,0:T(8,128)(2,1)}, s32[128]{0:T(128)S(1)}, s32[2,512]{1,0:T(2,128)S(1)}, /*i...) while((s32[]{:T(128)}, f32[128,16,72]{0,2,1:T(8,128)}, ...), condition=%wide.region_10.11_spmd.clone, body=%wide.region_9.10_spmd.clone.sunk | while | flops 459636736 | bytes 13852814 | solution.py:118
  136.4 5.8 %fusion.126 = f32[128,16,72]{0,2,1:T(8,128)} fusion(f32[16,512,128]{2,1,0:T(8,128)} %fusion.125, bf16[128,16,72]{0,2,1:T(8,128)(2,1)} %get-tuple-element.861, f32[16,128]{1,0:T(8,128)S(1)} %bitcast.249, f32[16,128]{1,0:T(8,128)S(1)} %get-tuple-element.859, pred[128,512]{0,1:T(8,128)(4,1)S(1)} %broadcast_compare_fusion.10, ...), kind=kOutput, calls=%fused_computation.34.clone.1 | convolution fusion | flops 308576256 | bytes 8111616 | tf_op jit(solution)/shard_map/while/body/eval_jaxpr/hqk,khd->qhd/dot_general | solution.py:114
  146.5 5.9 %fusion.126 = f32[128,16,72]{0,2,1:T(8,128)} fusion(f32[16,512,128]{2,1,0:T(8,128)} %fusion.125, bf16[128,16,72]{0,2,1:T(8,128)(2,1)} %get-tuple-element.861, f32[16,128]{1,0:T(8,128)S(1)} %bitcast.249, f32[16,128]{1,0:T(8,128)S(1)} %get-tuple-element.859, pred[128,512]{0,1:T(8,128)(4,1)S(1)} %broadcast_compare_fusion.10, ...), kind=kOutput, calls=%fused_computation.34.clone.1 | convolution fusion | flops 308576256 | bytes 8111616 | tf_op jit(solution)/shard_map/while/body/eval_jaxpr/hqk,khd->qhd/dot_general | solution.py:114
  154.4 9.6 %reshape.218 = bf16[2,512,16,72]{3,2,1,0:T(8,128)(2,1)} reshape(bf16[1024,1152]{1,0:T(8,128)(2,1)} %all-gather.9.cloned.1.call-done) | data formatting | bytes 4718592 | tf_op jit(solution)/shard_map/reshape | solution.py:124
  163.9 7.2 %copy.94 = bf16[2,512,16,72]{1,3,2,0:T(8,128)(2,1)} copy(bf16[2,512,16,72]{3,2,1,0:T(8,128)(2,1)} %reshape.218) | data formatting | bytes 4718592
  171.1 14.1 %all_gather.21 = f32[1024,16]{0,1:T(8,128)S(1)} all-gather(f32[128,16]{0,1:T(8,128)S(1)} %bitcast.250), channel_id=1, replica_groups=mesh['dp'=4,'seq'=8] {'seq'}, dimensions={0}, use_global_device_ids=true | all-gather | bytes 73728 | tf_op jit(solution)/shard_map/all_gather | solution.py:96
  185.3 14.2 %all_gather.23 = f32[1024,16]{0,1:T(8,128)S(1)} all-gather(f32[128,16]{0,1:T(8,128)S(1)} %get-tuple-element.939), channel_id=1, replica_groups=mesh['dp'=4,'seq'=8] {'seq'}, dimensions={0}, use_global_device_ids=true | all-gather | bytes 73728 | tf_op jit(solution)/shard_map/all_gather | solution.py:97
  199.5 9.6 %reshape.219 = bf16[2,512,16,72]{3,2,1,0:T(8,128)(2,1)} reshape(bf16[1024,1152]{1,0:T(8,128)(2,1)} %all-gather.11.cloned.1.call-done) | data formatting | bytes 4718592 | tf_op jit(solution)/shard_map/reshape | solution.py:125
  209.1 7.2 %copy.96 = bf16[2,512,16,72]{1,3,2,0:T(8,128)(2,1)} copy(bf16[2,512,16,72]{3,2,1,0:T(8,128)(2,1)} %reshape.219) | data formatting | bytes 4718592
  218.4 31.1 %while.51 = (s32[]{:T(128)}, f32[128,16,72]{0,2,1:T(8,128)}, f32[128,16,72]{0,2,1:T(8,128)}, bf16[2,512,16,72]{1,3,2,0:T(8,128)(2,1)}, s32[128]{0:T(128)S(1)}, /...) while((s32[]{:T(128)}, f32[128,16,72]{0,2,1:T(8,128)}, ...), condition=%wide.region_12.13_spmd.clone, body=%wide.region_11.12_spmd.clone.sunk | while | flops 615120896 | bytes 20816032 | solution.py:151
  222.7 6.9 %fusion.135 = f32[128,16,72]{0,2,1:T(8,128)} fusion(f32[16,512,128]{2,1,0:T(8,128)} %fusion.134, bf16[128,16,72]{0,2,1:T(8,128)(2,1)S(1)} %get-tuple-element.900, f32[16,512]{1,0:T(8,128)S(1)} %bitcast.241, f32[16,512]{1,0:T(8,128)S(1)} %bitcast.239, pred[128,512]{0,1:T(8,128)(4,1)S(1)} %broadcast_compare_fusion.11, ...), kind=kOutput, calls=%fused_computation.61.clone.1 | convolution fusion | flops 308576256 | bytes 8160768 | tf_op jit(solution)/shard_map/while/body/eval_jaxpr/hkq,qhd->khd/dot_general | solution.py:145
  229.5 4.4 %fusion.136 = f32[128,16,72]{0,2,1:T(8,128)} fusion(f32[16,512,128]{2,1,0:T(8,128)} %fusion.134, f32[16,512]{1,0:T(8,128)S(1)} %bitcast.240, pred[128,512]{0,1:T(8,128)(4,1)S(1)} %broadcast_compare_fusion.11, bf16[2,512,16,72]{1,3,2,0:T(8,128)(2,1)} %get-tuple-element.899, s32[]{:T(128)S(6)} %copy.149, f32[128,16,72]{0,2,1:T(8,128)} %get-tuple-element.880, ...), kind=kOutput, calls=%fused_computation.60.clone.1 | convolution fusion | flops 155484160 | bytes 6651909 | tf_op jit(solution)/shard_map/while/body/eval_jaxpr/hkq,qhd->khd/dot_general | solution.py:138
  238.2 6.8 %fusion.135 = f32[128,16,72]{0,2,1:T(8,128)} fusion(f32[16,512,128]{2,1,0:T(8,128)} %fusion.134, bf16[128,16,72]{0,2,1:T(8,128)(2,1)S(1)} %get-tuple-element.900, f32[16,512]{1,0:T(8,128)S(1)} %bitcast.241, f32[16,512]{1,0:T(8,128)S(1)} %bitcast.239, pred[128,512]{0,1:T(8,128)(4,1)S(1)} %broadcast_compare_fusion.11, ...), kind=kOutput, calls=%fused_computation.61.clone.1 | convolution fusion | flops 308576256 | bytes 8160768 | tf_op jit(solution)/shard_map/while/body/eval_jaxpr/hkq,qhd->khd/dot_general | solution.py:145
  245.0 4.5 %fusion.136 = f32[128,16,72]{0,2,1:T(8,128)} fusion(f32[16,512,128]{2,1,0:T(8,128)} %fusion.134, f32[16,512]{1,0:T(8,128)S(1)} %bitcast.240, pred[128,512]{0,1:T(8,128)(4,1)S(1)} %broadcast_compare_fusion.11, bf16[2,512,16,72]{1,3,2,0:T(8,128)(2,1)} %get-tuple-element.899, s32[]{:T(128)S(6)} %copy.149, f32[128,16,72]{0,2,1:T(8,128)} %get-tuple-element.880, ...), kind=kOutput, calls=%fused_computation.60.clone.1 | convolution fusion | flops 155484160 | bytes 6651909 | tf_op jit(solution)/shard_map/while/body/eval_jaxpr/hkq,qhd->khd/dot_general | solution.py:138
  (93 shorter events, 61.6 us)
Async XLA Ops:
  7.2 111.4 %copy-start = (bf16[1152,1152]{1,0:T(8,128)(2,1)S(1)}, bf16[1152,1152]{1,0:T(8,128)(2,1)}, u32[]{:S(2)}) copy-start(bf16[1152,1152]{1,0:T(8,128)(2,1)} %param.18) | copy-start | bytes 7962628
  7.2 36.8 %all-gather.5.cloned.1.call-start = ((), (), s32[]{:S(2)}) async-start(), calls=%async_computation.2 | async-start | bytes 2654208 | tf_op jit(solution)/shard_map/all_gather | solution.py:31
  7.9 68.5 %all-gather.7.cloned.1.call-start = ((), (), s32[]{:S(2)}) async-start(), calls=%async_computation.3 | async-start | bytes 2654208 | tf_op jit(solution)/shard_map/all_gather | solution.py:32
  8.7 145.7 %all-gather.9.cloned.1.call-start = ((), (), s32[]{:S(2)}) async-start(), calls=%async_computation.4 | async-start | bytes 2654208 | tf_op jit(solution)/shard_map/all_gather | solution.py:100
  9.4 190.1 %all-gather.11.cloned.1.call-start = ((), (), s32[]{:S(2)}) async-start(), calls=%async_computation.5 | async-start | bytes 2654208 | tf_op jit(solution)/shard_map/all_gather | solution.py:101
  108.1 10.4 %copy-start.2 = (bf16[128,1152]{1,0:T(8,128)(2,1)S(1)}, bf16[128,1152]{1,0:T(8,128)(2,1)}, u32[]{:S(2)}) copy-start(bf16[128,1152]{1,0:T(8,128)(2,1)} %param.17) | copy-start | bytes 884740
  121.3 6.8 %copy-start.1 = (bf16[128,1152]{1,0:T(8,128)(2,1)S(1)}, bf16[128,1152]{1,0:T(8,128)(2,1)}, u32[]{:S(2)}) copy-start(bf16[128,1152]{1,0:T(8,128)(2,1)} %get-tuple-element.543) | copy-start | bytes 884740
  121.4 95.0 %reduce-scatter.5.cloned.1.call-start = ((), (), s32[]{:S(2)}) async-start(), calls=%async_computation.6 | async-start | bytes 2985984 | tf_op jit(solution)/shard_map/reduce_scatter | solution.py:161
  124.8 128.7 %reduce-scatter.7.cloned.1.call-start = ((), (), s32[]{:S(2)}) async-start(), calls=%async_computation.7 | async-start | bytes 737280
  209.1 9.2 %copy-start.3 = (bf16[128,1152]{0,1:T(8,128)(2,1)S(1)}, bf16[128,1152]{0,1:T(8,128)(2,1)}, u32[]{:S(2)}) copy-start(bf16[128,1152]{0,1:T(8,128)(2,1)} %copy.93) | copy-start | bytes 884740
Sparse Core Ops, SparseCore 0:
  9.7 34.3 all-gather.4
  45.6 30.7 all-gather.6
  78.1 30.7 all-gather.8
  121.5 30.8 all-gather.10
  154.6 36.9 reduce-scatter.4
  218.5 24.0 reduce-scatter.6
where the time goes:
time: 264 us; the launch traced here: 262 us
  local copies, waits for them, and re-layouts  81.3 us (31%)
  matrix products  73 us (28%)
  waiting for transfers between devices  50.1 us (19%)
  blocking collectives  28.3 us (11%)
  other arithmetic  14.5 us (5%)
  between operations  14.3 us (5%)
    unnamed x20, local copies, waits for them, and re-layouts  38.6 us
    all_gather x1, waiting for transfers between devices, local(): lax.all_gather(keys, 'seq', axis=0, tiled=True)  32.3 us
    dot_general x4, matrix products, query_scores(): jnp.einsum('qhd,khd->hqk', query_heads, key_block, preferred_element_type...  16.5 us
    all_gather x1, waiting for transfers between devices, local(): lax.all_gather(values, 'seq', axis=0, tiled=True)  15.7 us
    all_gather x1, blocking collectives, local(): lax.all_gather(delta_rows, 'seq', axis=0, tiled=True)  14.2 us
    all_gather x1, blocking collectives, local(): lax.all_gather(log_total.T, 'seq', axis=0, tiled=True)  14.1 us
    dot_general x2, matrix products, key_side(): jnp.einsum('hkq,qhd->khd', dscores, query_block, preferred_element_type=j...  13.7 us
    dot_general x2, matrix products, query_side(): jnp.einsum('hqk,khd->qhd', dscores, key_block, preferred_element_type=jnp...  11.7 us
  transfers between devices with their start and end apart: 6, of which 2 were waited for; matrix products, arithmetic and copies ran while one was open for 63% of the time, Pallas kernels for 0%

commit v1 on v0

v1 whole, which is shorter than its diff:
```python
import functools
import math

import jax
import jax.numpy as jnp
from jax import lax
from jax.experimental import pallas as pl
from jax.experimental.pallas import tpu as pltpu
from jax.sharding import PartitionSpec as P

HEADS = 16
HEAD = 72
UNIT = 64
BAND = 80
FAR = -float(2.0**60)
F32 = jnp.float32
BF16 = jnp.bfloat16
MESH = pl.DeviceIdType.MESH
NT = (((1,), (1,)), ((), ()))
NN = (((1,), (0,)), ((), ()))


def dot(a, b, dims=NN):
    return lax.dot_general(a, b, dims, preferred_element_type=F32)


def kernel(
    n, ndp, images, ext_ref, q_ref, k_ref, v_ref, og_ref, w_ref,
    dq_ref, dk_ref, dv_ref, dw_ref,
    og_all, w_mine, flip, send_a, send_b, recv_a, recv_b,
    ret_a, ret_b, back_a, back_b,
    xq, xk, xv, xd, kn, vn, do_t, att_t, dq_s, dk_s, dv_s, w_out, w_in,
    sem_sa, sem_ra, sem_sb, sem_rb, sem_ta, sem_ka, sem_tb, sem_kb,
    sem_og, sem_up, sem_down, sem_sib, sem_ws, sem_wr, sem_w,
):
    rows, width = q_ref.shape
    per = HEADS // n
    span = per * HEAD
    seq = n * rows
    two = per == 2
    low = 64 if two else BAND
    line = n // 2
    me = lax.axis_index("seq")
    dp = lax.axis_index("dp")
    z = me // 2
    core = lax.rem(me, 2)
    sib = me + 1 - 2 * core
    groups = width // rows

    if w_ref.shape[0] == span:
        w_copy = pltpu.make_async_copy(w_ref, w_mine, sem_w)
    else:
        at = pl.multiple_of(me * span, span)
        w_copy = pltpu.make_async_copy(w_ref.at[pl.ds(at, span), :], w_mine, sem_w)
    w_copy.start()

    barrier = pltpu.get_barrier_semaphore()
    for p in range(1, n):
        pl.semaphore_signal(
            barrier, inc=1, device_id={"seq": lax.rem(me + p, n)}, device_id_type=MESH
        )
    for p in range(1, ndp):
        pl.semaphore_signal(
            barrier, inc=1, device_id={"dp": lax.rem(dp + p, ndp)}, device_id_type=MESH
        )

    og_all[pl.ds(me, 1)] = og_ref[...][None]

    def pack(ref, which):
        for g in range(groups):
            part = ref[:, g * rows:(g + 1) * rows].astype(F32)
            flip[g * rows:(g + 1) * rows, :] = part.T
        for d in range(n):
            base = d * span
            if two:
                send_a[d, which * BAND:(which + 1) * BAND, :] = flip[base:base + BAND, :].astype(BF16)
                send_b[d, which * 64:(which + 1) * 64, :] = flip[base + BAND:base + span, :].astype(BF16)
            else:
                padded = jnp.concatenate(
                    [flip[base:base + span, :], jnp.zeros((BAND - span, rows), F32)], axis=0
                )
                send_a[d, which * BAND:(which + 1) * BAND, :] = padded.astype(BF16)

    pack(q_ref, 0)
    pack(k_ref, 1)
    pack(v_ref, 2)
    pl.semaphore_wait(barrier, n - 1 + ndp - 1)

    def relay(src, send_sem, target):
        return pltpu.make_async_remote_copy(
            src_ref=og_all.at[src],
            dst_ref=og_all.at[src],
            send_sem=send_sem,
            recv_sem=sem_og.at[src],
            device_id={"seq": target},
            device_id_type=MESH,
        )

    def exchange(out, into, send_sem, recv_sem, peer, slot):
        return pltpu.make_async_remote_copy(
            src_ref=out.at[peer],
            dst_ref=into.at[slot],
            send_sem=send_sem.at[peer],
            recv_sem=recv_sem.at[slot],
            device_id={"seq": peer},
            device_id_type=MESH,
        )

    def send_all(out, into, send_sem, recv_sem):
        @pl.loop(1, n)
        def _(p):
            exchange(out, into, send_sem, recv_sem, lax.rem(me + p, n), me).start()

    def wait_all(out, into, send_sem, recv_sem):
        @pl.loop(1, n)
        def _(p):
            peer = lax.rem(me + p, n)
            exchange(out, into, send_sem, recv_sem, peer, peer).wait_recv()

    def wait_sent(out, into, send_sem, recv_sem):
        @pl.loop(1, n)
        def _(p):
            peer = lax.rem(me + p, n)
            exchange(out, into, send_sem, recv_sem, peer, peer).wait_send()

    can_up = z < line - 1
    can_down = z > 0

    @pl.when(can_up)
    def _():
        relay(me, sem_up.at[z], me + 2).start()

    @pl.when(can_down)
    def _():
        relay(me, sem_down.at[z], me - 2).start()

    relay(me, sem_sib.at[z], sib).start()
    set_a = (send_a, recv_a, sem_sa, sem_ra)
    set_b = (send_b, recv_b, sem_sb, sem_rb)
    send_all(*set_a)
    recv_a[pl.ds(me, 1)] = send_a[pl.ds(me, 1)]
    if two:
        recv_b[pl.ds(me, 1)] = send_b[pl.ds(me, 1)]

    for step in range(1, line):
        @pl.when(z >= step)
        def _():
            src = me - 2 * step
            relay(src, sem_up.at[z - step], sib).wait_recv()

            @pl.when(can_up)
            def _():
                relay(src, sem_up.at[z - step], me + 2).start()

            relay(src, sem_sib.at[z - step], sib).start()

        @pl.when(z + step < line)
        def _():
            src = me + 2 * step
            relay(src, sem_down.at[z + step], sib).wait_recv()

            @pl.when(can_down)
            def _():
                relay(src, sem_down.at[z + step], me - 2).start()

            relay(src, sem_sib.at[z + step], sib).start()

        if step == 1 and two:
            send_all(*set_b)

    for other in range(line):
        relay(2 * other + 1 - core, sem_sib.at[other], sib).wait_recv()
    w_copy.wait()

    @pl.loop(0, n)
    def _(s):
        lanes = pl.ds(pl.multiple_of(s * rows, rows), rows)
        do_t[0:span, lanes] = dot(w_mine[...], og_all[s], NT)

    ends = []
    total = jnp.int32(0)
    for i in range(images):
        total = total + ext_ref[0, i] * UNIT
        ends.append(total)

    block = math.gcd(seq, 256)
    scale = HEAD ** (-0.5)
    turn = scale * math.log2(math.e)

    def head(h):
        first = 0 if h == 0 else 8
        feature = HEAD if h == 0 else 0
        off = 64 * h
        row = lax.broadcasted_iota(jnp.int32, (BAND, rows), 0)
        own = (row >= first) & (row < first + HEAD)
        for s in range(n):
            spot = lax.broadcasted_iota(jnp.int32, (BAND, rows), 1) + s * rows
            segment = jnp.zeros((BAND, rows), jnp.int32)
            for end in ends:
                segment = segment + (spot >= end).astype(jnp.int32)
            hit = (row - feature) == segment
            lanes = slice(s * rows, (s + 1) * rows)

            def take(which):
                if h == 0:
                    return recv_a[s, which * BAND:(which + 1) * BAND, :].astype(F32)
                return jnp.concatenate(
                    [
                        recv_a[s, which * BAND + 64:(which + 1) * BAND, :].astype(F32),
                        recv_b[s, which * 64:(which + 1) * 64, :].astype(F32),
                    ],
                    axis=0,
                )

            qs = jnp.where(own, take(0), jnp.where(hit, 1.0, 0.0))
            ks = jnp.where(own, take(1), jnp.where(hit, 0.0, FAR))
            vs = jnp.where(own, take(2), 0.0)
            xq[:, lanes] = qs.astype(BF16)
            xk[:, lanes] = ks.astype(BF16)
            xv[:, lanes] = vs.astype(BF16)
            kn[lanes, :] = ks.T.astype(BF16)
            vn[lanes, :] = vs.T.astype(BF16)
            xd[:, lanes] = jnp.where(own, do_t[off:off + BAND, lanes], 0.0).astype(BF16)

        dk_s[...] = jnp.zeros_like(dk_s)
        dv_s[...] = jnp.zeros_like(dv_s)

        @pl.loop(0, seq // block)
        def _(b):
            lanes = pl.ds(pl.multiple_of(b * block, block), block)
            q = xq[:, lanes]
            back = xd[:, lanes]
            scores = dot(kn[...], q)
            top = jnp.max(scores, axis=0, keepdims=True)
            grown = jnp.exp2((scores - top) * turn)
            inverse = 1.0 / jnp.sum(grown, axis=0, keepdims=True)
            probs = grown * inverse
            probs_low = probs.astype(BF16)
            attended = dot(xv[...], probs_low).astype(BF16).astype(F32)
            delta = jnp.sum(back.astype(F32) * attended, axis=0, keepdims=True)
            dprobs = dot(vn[...], back)
            dscores = (probs * (dprobs - delta)).astype(BF16)
            dq_s[:, lanes] = dot(xk[...], dscores) * scale
            dk_s[...] += dot(q, dscores, NT)
            dv_s[...] += dot(back, probs_low, NT)
            if h == 0:
                att_t[0:BAND, lanes] = attended
            else:
                att_t[72:80, lanes] = attended[8:16]
                att_t[80:144, lanes] = attended[16:80]

        for s in range(n):
            lanes = slice(s * rows, (s + 1) * rows)
            for which, ref in enumerate((dq_s, dk_s, dv_s)):
                part = ref[:, lanes]
                if which == 1:
                    part = part * scale
                if h == 0:
                    ret_a[s, which * low:(which + 1) * low, :] = part[0:low].astype(BF16)
                    if two:
                        ret_b[s, which * BAND:which * BAND + 16, :] = part[64:80].astype(BF16)
                else:
                    old = ret_b[s, which * BAND:which * BAND + 16, :].astype(F32)
                    part = jnp.concatenate([old[0:8], part[8:80]], axis=0)
                    ret_b[s, which * BAND:(which + 1) * BAND, :] = part.astype(BF16)

    wait_all(*set_a)
    head(0)
    set_ra = (ret_a, back_a, sem_ta, sem_ka)
    set_rb = (ret_b, back_b, sem_tb, sem_kb)
    send_all(*set_ra)
    back_a[pl.ds(me, 1)] = ret_a[pl.ds(me, 1)]
    if two:
        wait_all(*set_b)
        head(1)
        send_all(*set_rb)
        back_b[pl.ds(me, 1)] = ret_b[pl.ds(me, 1)]

    piece = width // ndp
    term = jnp.zeros((span, width), F32)
    term = dot(att_t[0:span, :].astype(BF16), og_all[...].reshape(seq, width))
    for j in range(ndp):
        w_out[j, 0:span, :] = term[:, j * piece:(j + 1) * piece].astype(BF16)

    def reduce_copy(peer, slot):
        return pltpu.make_async_remote_copy(
            src_ref=w_out.at[peer],
            dst_ref=w_in.at[slot],
            send_sem=sem_ws.at[peer],
            recv_sem=sem_wr.at[slot],
            device_id={"dp": peer},
            device_id_type=MESH,
        )

    for p in range(1, ndp):
        reduce_copy(lax.rem(dp + p, ndp), dp).start()
    w_in[pl.ds(dp, 1)] = w_out[pl.ds(dp, 1)]
    for p in range(1, ndp):
        peer = lax.rem(dp + p, ndp)
        reduce_copy(peer, peer).wait_recv()
    result = w_in[0, 0:span, :].astype(F32)
    for j in range(1, ndp):
        result = result + w_in[j, 0:span, :].astype(F32)
    dw_ref[...] = result

    wait_all(*set_ra)
    if two:
        wait_all(*set_rb)
    for which, out in enumerate((dq_ref, dk_ref, dv_ref)):
        for d in range(n):
            base = d * span
            first = back_a[d, which * low:(which + 1) * low, :].astype(F32)
            if two:
                flip[base:base + 64, :] = first
                flip[base + 64:base + span, :] = back_b[
                    d, which * BAND:(which + 1) * BAND, :
                ].astype(F32)
            else:
                flip[base:base + span, :] = first[0:span]
        for g in range(groups):
            out[:, g * rows:(g + 1) * rows] = flip[g * rows:(g + 1) * rows, :].T.astype(BF16)

    wait_sent(*set_a)
    wait_sent(*set_ra)
    if two:
        wait_sent(*set_b)
        wait_sent(*set_rb)
    for p in range(1, ndp):
        peer = lax.rem(dp + p, ndp)
        reduce_copy(peer, peer).wait_send()
    for part in range(line):
        relay(2 * part + core, sem_sib.at[part], sib).wait_send()

        @pl.when(can_up & (z >= part))
        def _():
            relay(2 * part + core, sem_up.at[part], sib).wait_send()

        @pl.when(can_down & (z <= part))
        def _():
            relay(2 * part + core, sem_down.at[part], sib).wait_send()


def local(n, ndp, queries, keys, values, out_grad, out_weight, extents):
    rows, width = queries.shape
    per = HEADS // n
    assert per in (1, 2) and rows % 128 == 0
    span = per * HEAD
    padded = -(-span // 16) * 16
    seq = n * rows
    line = n // 2
    images = extents.shape[1]
    low = 64 if per == 2 else BAND
    if span % 16:
        out_weight = lax.dynamic_slice_in_dim(
            out_weight, lax.axis_index("seq") * span, span, axis=0
        )
    vmem = pl.BlockSpec(memory_space=pltpu.VMEM)
    grad = jax.ShapeDtypeStruct((rows, width), BF16)
    dma = pltpu.SemaphoreType.DMA
    buf = pltpu.VMEM
    return pl.pallas_call(
        functools.partial(kernel, n, ndp, images),
        out_shape=(grad, grad, grad, jax.ShapeDtypeStruct((span, width // ndp), F32)),
        in_specs=[
            pl.BlockSpec(memory_space=pltpu.SMEM), vmem, vmem, vmem, vmem,
            pl.BlockSpec(memory_space=pl.ANY),
        ],
        out_specs=(vmem, vmem, vmem, vmem),
        scratch_shapes=[
            buf((n, rows, width), BF16),
            buf((span, width), BF16),
            buf((width, rows), F32),
            buf((n, 3 * BAND, rows), BF16),
            buf((n, 3 * 64, rows), BF16),
            buf((n, 3 * BAND, rows), BF16),
            buf((n, 3 * 64, rows), BF16),
            buf((n, 3 * low, rows), BF16),
            buf((n, 3 * BAND, rows), BF16),
            buf((n, 3 * low, rows), BF16),
            buf((n, 3 * BAND, rows), BF16),
            buf((BAND, seq), BF16),
            buf((BAND, seq), BF16),
            buf((BAND, seq), BF16),
            buf((BAND, seq), BF16),
            buf((seq, BAND), BF16),
            buf((seq, BAND), BF16),
            buf((padded, seq), F32),
            buf((padded, seq), F32),
            buf((BAND, seq), F32),
            buf((BAND, seq), F32),
            buf((BAND, seq), F32),
            buf((ndp, padded, width // ndp), BF16),
            buf((ndp, padded, width // ndp), BF16),
        ]
        + [dma((n,))] * 8
        + [dma((n,)), dma((line,)), dma((line,)), dma((line,)), dma((ndp,)), dma((ndp,)), dma],
        compiler_params=pltpu.CompilerParams(
            collective_id=0, has_side_effects=True, vmem_limit_bytes=48 * 2**20
        ),
        cost_estimate=pl.CostEstimate(
            flops=10 * per * seq * seq * HEAD, bytes_accessed=10 * rows * width * 2,
            transcendentals=per * seq * seq,
        ),
    )(extents, queries, keys, values, out_grad, out_weight)


def solution(mesh):
    n, ndp = mesh.shape["seq"], mesh.shape["dp"]
    return jax.shard_map(
        functools.partial(local, n, ndp),
        mesh=mesh,
        in_specs=(
            P(("dp", "seq"), None),
            P(("dp", "seq"), None),
            P(("dp", "seq"), None),
            P(("dp", "seq"), None),
            P(),
            P("dp", None),
        ),
        out_specs=(
            P(("dp", "seq"), None),
            P(("dp", "seq"), None),
            P(("dp", "seq"), None),
            P("seq", "dp"),
        ),
        check_vma=False,
    )
```

time: 264 us -> 80.1 us (0.30)
  matrix products: 73 us -> 0 us
  local copies, waits for them, and re-layouts: 81.3 us -> 9.07 us
  Pallas kernels: 0 us -> 69.7 us
  waiting for transfers between devices: 50.1 us -> 0 us
  blocking collectives: 28.3 us -> 0 us
  other arithmetic: 14.5 us -> 0 us
  between operations: 14.3 us -> 0.66 us
    dot_general x16 -> x0, matrix products: 73 us -> none  [the longest x4 16.5 us: query_scores(): jnp.einsum('qhd,khd->hqk', query_heads, key_block, preferred_element_type...]
    pallas_call x0 -> x1, Pallas kernels: none -> 69.7 us  [local(): pl.pallas_call(functools.partial(kernel, n, ndp, images), out_shape=(grad...]
    all_gather x4 -> x0, waiting for transfers between devices: 48 us -> none  [the longest x1 32.3 us: local(): lax.all_gather(keys, 'seq', axis=0, tiled=True)]
    reshape x8 -> x0, local copies, waits for them, and re-layouts: 39.4 us -> none  [the longest x1 9.6 us: local(): back_blocks = back_all.reshape(num_blocks, block_len, HEADS, HEAD)]
    unnamed x20 -> x16, local copies, waits for them, and re-layouts: 38.6 us -> 9.07 us
    all_gather x2 -> x0, blocking collectives: 28.3 us -> none  [the longest x1 14.2 us: local(): lax.all_gather(delta_rows, 'seq', axis=0, tiled=True)]
    reduce_sum x4 -> x0, other arithmetic: 7.36 us -> none  [the longest x2 6.16 us: grow_total(): jnp.sum(jnp.where(inside, jnp.exp(scores - top_next[:, :, None]), 0.0), a...]
    convert_element_type x5 -> x0, other arithmetic: 5.17 us -> none  [the longest x1 1.13 us: local(): (query_acc * score_scale).astype(jnp.bfloat16)]
  transfers between devices with their start and end apart: 6 -> 0, of which waited for: 2 -> 0; matrix products, arithmetic and copies ran while one was open for 63% -> 0% of each run, Pallas kernels for 0% -> 0%
where the time goes in v1:
time: 80.1 us; the launch traced here: 79.4 us
  Pallas kernels  69.7 us (87%)
  local copies, waits for them, and re-layouts  9.07 us (11%)
    pallas_call x1, Pallas kernels, local(): pl.pallas_call(functools.partial(kernel, n, ndp, images), out_shape=(grad...  69.7 us
    unnamed x16, local copies, waits for them, and re-layouts  9.07 us

profile of v1, /device:TPU:0, one launch (start us, length us, event | category | flops | bytes accessed | tf_op | source)
XLA Modules:
  0.0 79.4 jit_solution(16427611353537059205)
XLA Ops:
  0.6 0.0 copy-start
  0.6 1.7 %copy-done = bf16[1152,1152]{1,0:T(8,128)(2,1)S(1)} copy-done((bf16[1152,1152]{1,0:T(8,128)(2,1)S(1)}, bf16[1152,1152]{1,0:T(8,128)(2,1)}, u32[]{:S(2)}) %copy-start) | copy-done | bytes 2654232
  2.4 0.0 copy-start.1
  2.4 1.0 %copy-done.1 = bf16[128,1152]{1,0:T(8,128)(2,1)S(1)} copy-done((bf16[128,1152]{1,0:T(8,128)(2,1)S(1)}, bf16[128,1152]{1,0:T(8,128)(2,1)}, u32[]{:S(2)}) %copy-start.1) | copy-done | bytes 294936
  3.3 0.0 copy-start.2
  3.3 1.0 %copy-done.2 = bf16[128,1152]{1,0:T(8,128)(2,1)S(1)} copy-done((bf16[128,1152]{1,0:T(8,128)(2,1)S(1)}, bf16[128,1152]{1,0:T(8,128)(2,1)}, u32[]{:S(2)}) %copy-start.2) | copy-done | bytes 294936
  4.3 0.0 copy-start.3
  4.3 1.0 %copy-done.3 = bf16[128,1152]{1,0:T(8,128)(2,1)S(1)} copy-done((bf16[128,1152]{1,0:T(8,128)(2,1)S(1)}, bf16[128,1152]{1,0:T(8,128)(2,1)}, u32[]{:S(2)}) %copy-start.3) | copy-done | bytes 294936
  5.3 0.0 copy-start.4
  5.3 1.0 %copy-done.4 = bf16[128,1152]{1,0:T(8,128)(2,1)S(1)} copy-done((bf16[128,1152]{1,0:T(8,128)(2,1)S(1)}, bf16[128,1152]{1,0:T(8,128)(2,1)}, u32[]{:S(2)}) %copy-start.4) | copy-done | bytes 294936
  6.2 0.0 copy-start.5
  6.2 0.7 copy-done.5
  6.9 69.7 %shard_map.93 = (bf16[128,1152]{1,0:T(8,128)(2,1)S(1)}, bf16[128,1152]{1,0:T(8,128)(2,1)S(1)}, bf16[128,1152]{1,0:T(8,128)(2,1)S(1)}, f32[144,288]{1,0:T(8,128)S(1)}) custom-call(s32[1,8]{1,0:T(1,128)S(1)} %copy-done.5, bf16[128,1152]{1,0:T(8,128)(2,1)S(1)} %copy-done.1, bf16[128,1152]{1,0:T(8,128)(2,1)S(1)} %copy-done.2, bf16[128,1152]{1,0:T(8,128)(2,1)S(1)} %copy-done.3, ...), custom_call_target="tpu_custom_call" | custom-call | flops 1509949440 | bytes 2949120 | tf_op jit(solution)/shard_map/pallas_call | solution.py:361
  76.6 0.7 copy.14
  77.3 0.7 copy.15
  78.0 0.7 copy.16
  78.7 0.7 copy.17
Async XLA Ops:
  0.6 1.8 %copy-start = (bf16[1152,1152]{1,0:T(8,128)(2,1)S(1)}, bf16[1152,1152]{1,0:T(8,128)(2,1)}, u32[]{:S(2)}) copy-start(bf16[1152,1152]{1,0:T(8,128)(2,1)} %w_ref.1) | copy-start | bytes 7962628
  2.4 1.0 %copy-start.1 = (bf16[128,1152]{1,0:T(8,128)(2,1)S(1)}, bf16[128,1152]{1,0:T(8,128)(2,1)}, u32[]{:S(2)}) copy-start(bf16[128,1152]{1,0:T(8,128)(2,1)} %q_ref.1) | copy-start | bytes 884740
  3.3 1.0 %copy-start.2 = (bf16[128,1152]{1,0:T(8,128)(2,1)S(1)}, bf16[128,1152]{1,0:T(8,128)(2,1)}, u32[]{:S(2)}) copy-start(bf16[128,1152]{1,0:T(8,128)(2,1)} %k_ref.1) | copy-start | bytes 884740
  4.3 1.0 %copy-start.3 = (bf16[128,1152]{1,0:T(8,128)(2,1)S(1)}, bf16[128,1152]{1,0:T(8,128)(2,1)}, u32[]{:S(2)}) copy-start(bf16[128,1152]{1,0:T(8,128)(2,1)} %v_ref.1) | copy-start | bytes 884740
  5.3 1.0 %copy-start.4 = (bf16[128,1152]{1,0:T(8,128)(2,1)S(1)}, bf16[128,1152]{1,0:T(8,128)(2,1)}, u32[]{:S(2)}) copy-start(bf16[128,1152]{1,0:T(8,128)(2,1)} %og_ref.1) | copy-start | bytes 884740
  6.2 0.7 copy-start.5

commit v2 on v1

v2 whole, which is shorter than its diff:
```python
import functools
import math

import jax
import jax.numpy as jnp
from jax import lax
from jax.experimental import pallas as pl
from jax.experimental.pallas import tpu as pltpu
from jax.sharding import PartitionSpec as P

HEADS = 16
HEAD = 72
UNIT = 64
BAND = 80
FAR = -float(2.0**60)
F32 = jnp.float32
BF16 = jnp.bfloat16
MESH = pl.DeviceIdType.MESH
NT = (((1,), (1,)), ((), ()))
NN = (((1,), (0,)), ((), ()))


def dot(a, b, dims=NN):
    return lax.dot_general(a, b, dims, preferred_element_type=F32)


def kernel(
    n, ndp, images, ext_ref, q_hbm, k_hbm, v_hbm, og_hbm, w_ref,
    dq_ref, dk_ref, dv_ref, dw_ref,
    q_ref, k_ref, v_ref, og_all, w_mine, flip, send_a, send_b, recv_a, recv_b,
    ret_q, ret_kv, back_q, back_kv,
    xq, xk, xv, kn, vn, probs_all, att_t, dk_s, dv_s, w_out, w_in,
    sem_sa, sem_ra, sem_sb, sem_rb, sem_tq, sem_kq, sem_tk, sem_kk,
    sem_og, sem_up, sem_down, sem_sib, sem_ws, sem_wr, sem_in,
):
    rows, width = q_ref.shape
    per = HEADS // n
    span = per * HEAD
    seq = n * rows
    two = per == 2
    line = n // 2
    pair = 2 * rows
    me = lax.axis_index("seq")
    dp = lax.axis_index("dp")
    z = me // 2
    core = lax.rem(me, 2)
    sib = me + 1 - 2 * core
    groups = width // rows

    if w_ref.shape[0] == span:
        w_from = w_ref
    else:
        w_from = w_ref.at[pl.ds(pl.multiple_of(me * span, span), span), :]
    loads = [
        pltpu.make_async_copy(src, dst, sem_in.at[i])
        for i, (src, dst) in enumerate(
            [(og_hbm, og_all.at[me]), (q_hbm, q_ref), (k_hbm, k_ref), (v_hbm, v_ref), (w_from, w_mine)]
        )
    ]
    for load in loads:
        load.start()

    barrier = pltpu.get_barrier_semaphore()
    for p in range(1, n):
        pl.semaphore_signal(
            barrier, inc=1, device_id={"seq": lax.rem(me + p, n)}, device_id_type=MESH
        )
    for p in range(1, ndp):
        pl.semaphore_signal(
            barrier, inc=1, device_id={"dp": lax.rem(dp + p, ndp)}, device_id_type=MESH
        )

    def relay(src, send_sem, target):
        return pltpu.make_async_remote_copy(
            src_ref=og_all.at[src],
            dst_ref=og_all.at[src],
            send_sem=send_sem,
            recv_sem=sem_og.at[src],
            device_id={"seq": target},
            device_id_type=MESH,
        )

    def exchange(out, into, send_sem, recv_sem, peer, slot):
        return pltpu.make_async_remote_copy(
            src_ref=out.at[peer],
            dst_ref=into.at[slot],
            send_sem=send_sem.at[peer],
            recv_sem=recv_sem.at[slot],
            device_id={"seq": peer},
            device_id_type=MESH,
        )

    def send_all(out, into, send_sem, recv_sem):
        @pl.loop(1, n)
        def _(p):
            exchange(out, into, send_sem, recv_sem, lax.rem(me + p, n), me).start()

    def wait_all(out, into, send_sem, recv_sem):
        @pl.loop(1, n)
        def _(p):
            peer = lax.rem(me + p, n)
            exchange(out, into, send_sem, recv_sem, peer, peer).wait_recv()

    def wait_sent(out, into, send_sem, recv_sem):
        @pl.loop(1, n)
        def _(p):
            peer = lax.rem(me + p, n)
            exchange(out, into, send_sem, recv_sem, peer, peer).wait_send()

    set_a = (send_a, recv_a, sem_sa, sem_ra)
    set_b = (send_b, recv_b, sem_sb, sem_rb)
    set_q = (ret_q, back_q, sem_tq, sem_kq)
    set_kv = (ret_kv, back_kv, sem_tk, sem_kk)
    can_up = z < line - 1
    can_down = z > 0

    loads[1].wait()
    loads[2].wait()
    loads[3].wait()
    for which, ref in enumerate((q_ref, k_ref, v_ref)):
        for g in range(groups):
            part = ref[:, g * rows:(g + 1) * rows].astype(F32)
            flip[which, g * rows:(g + 1) * rows, :] = part.T
        for d in range(n):
            base = d * span
            if two:
                part = flip[which, base:base + BAND, :]
            else:
                part = jnp.concatenate(
                    [flip[which, base:base + span, :], jnp.zeros((BAND - span, rows), F32)], axis=0
                )
            send_a[d, which * BAND:(which + 1) * BAND, :] = part.astype(BF16)
    loads[0].wait()
    pl.semaphore_wait(barrier, n - 1 + ndp - 1)
    send_all(*set_a)

    @pl.when(can_up)
    def _():
        relay(me, sem_up.at[z], me + 2).start()

    @pl.when(can_down)
    def _():
        relay(me, sem_down.at[z], me - 2).start()

    relay(me, sem_sib.at[z], sib).start()
    recv_a[pl.ds(me, 1)] = send_a[pl.ds(me, 1)]
    if two:
        for which in range(3):
            for d in range(n):
                base = d * span
                send_b[d, which * 64:(which + 1) * 64, :] = flip[
                    which, base + BAND:base + span, :
                ].astype(BF16)
        send_all(*set_b)
        recv_b[pl.ds(me, 1)] = send_b[pl.ds(me, 1)]

    def relay_step(step):
        @pl.when(z >= step)
        def _():
            src = me - 2 * step
            relay(src, sem_up.at[z - step], sib).wait_recv()

            @pl.when(can_up)
            def _():
                relay(src, sem_up.at[z - step], me + 2).start()

            relay(src, sem_sib.at[z - step], sib).start()

        @pl.when(z + step < line)
        def _():
            src = me + 2 * step
            relay(src, sem_down.at[z + step], sib).wait_recv()

            @pl.when(can_down)
            def _():
                relay(src, sem_down.at[z + step], me - 2).start()

            relay(src, sem_sib.at[z + step], sib).start()

    ends = []
    total = jnp.int32(0)
    for i in range(images):
        total = total + ext_ref[0, i] * UNIT
        ends.append(total)

    scale = HEAD ** (-0.5)
    turn = scale * math.log2(math.e)

    def owned(h, lanes):
        row = lax.broadcasted_iota(jnp.int32, (BAND, lanes), 0)
        first = 0 if h == 0 else 8
        return (row >= first) & (row < first + HEAD)

    def forward(h):
        feature = HEAD if h == 0 else 0
        row = lax.broadcasted_iota(jnp.int32, (BAND, rows), 0)
        own = owned(h, rows)
        for s in range(n):
            spot = lax.broadcasted_iota(jnp.int32, (1, rows), 1) + s * rows
            segment = jnp.zeros((1, rows), jnp.int32)
            for end in ends:
                segment = segment + (spot >= end).astype(jnp.int32)
            hit = (row - feature) == segment
            lanes = slice(s * rows, (s + 1) * rows)

            def take(which):
                if h == 0:
                    return recv_a[s, which * BAND:(which + 1) * BAND, :].astype(F32)
                return jnp.concatenate(
                    [
                        recv_a[s, which * BAND + 64:(which + 1) * BAND, :].astype(F32),
                        recv_b[s, which * 64:(which + 1) * 64, :].astype(F32),
                    ],
                    axis=0,
                )

            qs = jnp.where(own, take(0), jnp.where(hit, 1.0, 0.0))
            ks = jnp.where(own, take(1), jnp.where(hit, 0.0, FAR))
            vs = jnp.where(own, take(2), 0.0)
            xq[h, :, lanes] = qs.astype(BF16)
            xk[h, :, lanes] = ks.astype(BF16)
            xv[h, :, lanes] = vs.astype(BF16)
            kn[h, lanes, :] = ks.T.astype(BF16)
            vn[h, lanes, :] = vs.T.astype(BF16)

        dk_s[h] = jnp.zeros((BAND, seq), F32)
        dv_s[h] = jnp.zeros((BAND, seq), F32)

        @pl.loop(0, line)
        def _(b):
            lanes = pl.ds(pl.multiple_of(b * pair, pair), pair)
            scores = dot(kn[h], xq[h, :, lanes])
            top = jnp.max(scores, axis=0, keepdims=True)
            grown = jnp.exp2((scores - top) * turn)
            inverse = 1.0 / jnp.sum(grown, axis=0, keepdims=True)
            probs = grown * inverse
            probs_all[h, :, lanes] = probs
            attended = dot(xv[h], probs.astype(BF16)).astype(BF16).astype(F32)
            if h == 0:
                att_t[0:BAND, lanes] = attended
            else:
                att_t[72:80, lanes] = attended[8:16]
                att_t[80:144, lanes] = attended[16:80]

    def backward(chip):
        lanes = pl.ds(pl.multiple_of(chip * pair, pair), pair)
        held = og_all[pl.ds(2 * chip, 2)].reshape(pair, width)
        backs = dot(w_mine[...], held, NT)
        if not two:
            backs = jnp.concatenate([backs, jnp.zeros((BAND - span, pair), F32)], axis=0)
        parts = []
        for h in range(per):
            off = 64 * h
            back = jnp.where(owned(h, pair), backs[off:off + BAND], 0.0).astype(BF16)
            delta = jnp.sum(
                back.astype(F32) * att_t[off:off + BAND, lanes], axis=0, keepdims=True
            )
            probs = probs_all[h, :, lanes]
            dprobs = dot(vn[h], back)
            dscores = (probs * (dprobs - delta)).astype(BF16)
            parts.append(dot(xk[h], dscores) * scale)
            dk_s[h] += dot(xq[h, :, lanes], dscores, NT)
            dv_s[h] += dot(back, probs.astype(BF16), NT)
        done = jnp.concatenate([parts[0][0:72], parts[1][8:80]], axis=0) if two else parts[0]
        for j in range(2):
            peer = 2 * chip + j
            block = done[:, j * rows:(j + 1) * rows].astype(BF16)
            ret_q[pl.ds(peer, 1)] = block[None]

            @pl.when(peer != me)
            def _():
                exchange(*set_q, peer, me).start()

    wait_all(*set_a)
    forward(0)
    relay_step(1)
    if two:
        wait_all(*set_b)
        forward(1)
    if line > 2:
        relay_step(2)
    loads[4].wait()
    near = jnp.minimum(z, line - 1 - z)
    toward = jnp.where(z < line - 1 - z, 1, -1)

    @pl.loop(0, line)
    def _(i):
        @pl.when((i >= 2) & (i + 1 < line))
        def _():
            relay_step(i + 1)

        swing = ((i + 1) // 2) * (1 - 2 * lax.rem(i, 2))
        chip = z + jnp.where(i <= 2 * near, swing, toward * (i - near))
        relay(2 * chip + 1 - core, sem_sib.at[chip], sib).wait_recv()
        backward(chip)

    tall = ret_q.shape[1]
    for s in range(n):
        lanes = slice(s * rows, (s + 1) * rows)
        for which, (ref, factor) in enumerate(((dk_s, scale), (dv_s, None))):
            if two:
                part = jnp.concatenate([ref[0, 0:72, lanes], ref[1, 8:80, lanes]], axis=0)
            else:
                part = ref[0, :, lanes]
            if factor is not None:
                part = part * factor
            ret_kv[s, which * tall:(which + 1) * tall, :] = part.astype(BF16)
    send_all(*set_kv)
    back_q[pl.ds(me, 1)] = ret_q[pl.ds(me, 1)]
    back_kv[pl.ds(me, 1)] = ret_kv[pl.ds(me, 1)]

    piece = width // ndp
    term = dot(att_t[0:span, :].astype(BF16), og_all[...].reshape(seq, width))
    for j in range(ndp):
        w_out[j, 0:span, :] = term[:, j * piece:(j + 1) * piece].astype(BF16)

    def reduce_copy(peer, slot):
        return pltpu.make_async_remote_copy(
            src_ref=w_out.at[peer],
            dst_ref=w_in.at[slot],
            send_sem=sem_ws.at[peer],
            recv_sem=sem_wr.at[slot],
            device_id={"dp": peer},
            device_id_type=MESH,
        )

    for p in range(1, ndp):
        reduce_copy(lax.rem(dp + p, ndp), dp).start()
    w_in[pl.ds(dp, 1)] = w_out[pl.ds(dp, 1)]

    def unpack(ref, first, out):
        for d in range(n):
            flip[0, d * span:(d + 1) * span, :] = ref[d, first:first + tall, :].astype(F32)[0:span]
        for g in range(groups):
            out[:, g * rows:(g + 1) * rows] = flip[0, g * rows:(g + 1) * rows, :].T.astype(BF16)

    wait_all(*set_q)
    unpack(back_q, 0, dq_ref)
    for p in range(1, ndp):
        peer = lax.rem(dp + p, ndp)
        reduce_copy(peer, peer).wait_recv()
    result = w_in[0, 0:span, :].astype(F32)
    for j in range(1, ndp):
        result = result + w_in[j, 0:span, :].astype(F32)
    dw_ref[...] = result
    wait_sent(*set_a)
    wait_sent(*set_q)
    if two:
        wait_sent(*set_b)
    for p in range(1, ndp):
        peer = lax.rem(dp + p, ndp)
        reduce_copy(peer, peer).wait_send()
    for part in range(line):
        relay(2 * part + core, sem_sib.at[part], sib).wait_send()

        @pl.when(can_up & (z >= part))
        def _():
            relay(2 * part + core, sem_up.at[part], sib).wait_send()

        @pl.when(can_down & (z <= part))
        def _():
            relay(2 * part + core, sem_down.at[part], sib).wait_send()

    wait_all(*set_kv)
    unpack(back_kv, 0, dk_ref)
    unpack(back_kv, tall, dv_ref)
    wait_sent(*set_kv)


def finish(*refs):
    count = len(refs) // 2
    sems = refs[-1]
    copies = [
        pltpu.make_async_copy(refs[i], refs[count + i], sems.at[i]) for i in range(count)
    ]
    for copy in copies:
        copy.start()
    for copy in copies:
        copy.wait()


def local(n, ndp, queries, keys, values, out_grad, out_weight, extents):
    rows, width = queries.shape
    per = HEADS // n
    assert per in (1, 2) and rows % 128 == 0
    span = per * HEAD
    padded = -(-span // 16) * 16
    seq = n * rows
    line = n // 2
    images = extents.shape[1]
    if span % 16:
        out_weight = lax.dynamic_slice_in_dim(
            out_weight, lax.axis_index("seq") * span, span, axis=0
        )
    vmem = pl.BlockSpec(memory_space=pltpu.VMEM)
    hbm = pl.BlockSpec(memory_space=pl.ANY)
    grad = jax.ShapeDtypeStruct((rows, width), BF16)
    weight = jax.ShapeDtypeStruct((span, width // ndp), F32)
    dma = pltpu.SemaphoreType.DMA
    buf = pltpu.VMEM
    parts = pl.pallas_call(
        functools.partial(kernel, n, ndp, images),
        out_shape=(grad, grad, grad, weight),
        in_specs=[pl.BlockSpec(memory_space=pltpu.SMEM), hbm, hbm, hbm, hbm, hbm],
        out_specs=(vmem, vmem, vmem, vmem),
        scratch_shapes=[
            buf((rows, width), BF16),
            buf((rows, width), BF16),
            buf((rows, width), BF16),
            buf((n, rows, width), BF16),
            buf((span, width), BF16),
            buf((3, width, rows), F32),
            buf((n, 3 * BAND, rows), BF16),
            buf((n, 3 * 64, rows), BF16),
            buf((n, 3 * BAND, rows), BF16),
            buf((n, 3 * 64, rows), BF16),
            buf((n, padded, rows), BF16),
            buf((n, 2 * padded, rows), BF16),
            buf((n, padded, rows), BF16),
            buf((n, 2 * padded, rows), BF16),
            buf((per, BAND, seq), BF16),
            buf((per, BAND, seq), BF16),
            buf((per, BAND, seq), BF16),
            buf((per, seq, BAND), BF16),
            buf((per, seq, BAND), BF16),
            buf((per, seq, seq), F32),
            buf((padded, seq), F32),
            buf((per, BAND, seq), F32),
            buf((per, BAND, seq), F32),
            buf((ndp, padded, width // ndp), BF16),
            buf((ndp, padded, width // ndp), BF16),
        ]
        + [dma((n,))] * 8
        + [dma((n,)), dma((line,)), dma((line,)), dma((line,)), dma((ndp,)), dma((ndp,)), dma((5,))],
        compiler_params=pltpu.CompilerParams(
            collective_id=0, has_side_effects=True, vmem_limit_bytes=56 * 2**20
        ),
        cost_estimate=pl.CostEstimate(
            flops=10 * per * seq * seq * HEAD, bytes_accessed=10 * rows * width * 2,
            transcendentals=per * seq * seq,
        ),
    )(extents, queries, keys, values, out_grad, out_weight)
    return pl.pallas_call(
        finish,
        out_shape=(grad, grad, grad, weight),
        in_specs=[hbm] * 4,
        out_specs=(hbm, hbm, hbm, hbm),
        scratch_shapes=[dma((4,))],
        compiler_params=pltpu.CompilerParams(vmem_limit_bytes=56 * 2**20),
    )(*parts)


def solution(mesh):
    n, ndp = mesh.shape["seq"], mesh.shape["dp"]
    return jax.shard_map(
        functools.partial(local, n, ndp),
        mesh=mesh,
        in_specs=(
            P(("dp", "seq"), None),
            P(("dp", "seq"), None),
            P(("dp", "seq"), None),
            P(("dp", "seq"), None),
            P(),
            P("dp", None),
        ),
        out_specs=(
            P(("dp", "seq"), None),
            P(("dp", "seq"), None),
            P(("dp", "seq"), None),
            P("seq", "dp"),
        ),
        check_vma=False,
    )
```

time: 80.1 us -> 102 us (1.27); the launches traced: 79.4 us -> 100 us
  Pallas kernels: 69.7 us -> 99.7 us
  local copies, waits for them, and re-layouts: 9.07 us -> 0 us
    pallas_call x0 -> x1, Pallas kernels: none -> 34.6 us  [local(): pl.pallas_call(finish, out_shape=(grad, grad, grad, weight), in_specs=[hb...]
    unnamed x16 -> x0, local copies, waits for them, and re-layouts: 9.07 us -> none
    pallas_call x1, Pallas kernels: 69.7 us -> 65 us  [local(): pl.pallas_call(functools.partial(kernel, n, ndp, images), out_shape=(grad...]
where the time goes in v2:
time: 102 us; the launch traced here: 100 us
  Pallas kernels  99.7 us (98%)
    pallas_call x1, Pallas kernels, local(): pl.pallas_call(functools.partial(kernel, n, ndp, images), out_shape=(grad...  65 us
    pallas_call x1, Pallas kernels, local(): pl.pallas_call(finish, out_shape=(grad, grad, grad, weight), in_specs=[hb...  34.6 us

profile of v2, /device:TPU:0, one launch (start us, length us, event | category | flops | bytes accessed | tf_op | source)
XLA Modules:
  0.0 100.3 jit_solution(3211507503774880366)
XLA Ops:
  0.6 65.0 %shard_map.93 = (bf16[128,1152]{1,0:T(8,128)(2,1)}, bf16[128,1152]{1,0:T(8,128)(2,1)}, bf16[128,1152]{1,0:T(8,128)(2,1)}, f32[144,288]{1,0:T(8,128)}) custom-call(s32[1,8]{1,0:T(1,128)} %ext_ref.1, bf16[128,1152]{1,0:T(8,128)(2,1)} %q_hbm.1, bf16[128,1152]{1,0:T(8,128)(2,1)} %k_hbm.1, bf16[128,1152]{1,0:T(8,128)(2,1)} %v_hbm.1, bf16[128,1152]{1,0:T(8,128)(2,1)} %og_hbm.1, ...), custom_call_target="tpu_custom_call" | custom-call | flops 1509949440 | bytes 2949120 | tf_op jit(solution)/shard_map/pallas_call | solution.py:401
  65.7 34.6 %shard_map.94 = (bf16[128,1152]{1,0:T(8,128)(2,1)}, bf16[128,1152]{1,0:T(8,128)(2,1)}, bf16[128,1152]{1,0:T(8,128)(2,1)}, f32[144,288]{1,0:T(8,128)}) custom-call(bf16[128,1152]{1,0:T(8,128)(2,1)} %get-tuple-element.8.refs_0_, bf16[128,1152]{1,0:T(8,128)(2,1)} %get-tuple-element.9.refs_1_, bf16[128,1152]{1,0:T(8,128)(2,1)} %get-tuple-element.10.refs_2_, ...), custom_call_target="tpu_custom_call" | custom-call | tf_op jit(solution)/shard_map/pallas_call | solution.py:443

commit v3 on v2

--- a/solution.py
+++ b/solution.py
@@ -28,9 +28,9 @@
     n, ndp, images, ext_ref, q_hbm, k_hbm, v_hbm, og_hbm, w_ref,
     dq_ref, dk_ref, dv_ref, dw_ref,
     q_ref, k_ref, v_ref, og_all, w_mine, flip, send_a, send_b, recv_a, recv_b,
-    ret_q, ret_kv, back_q, back_kv,
+    ret_q, ret_k, ret_v, back_q, back_k, back_v,
     xq, xk, xv, kn, vn, probs_all, att_t, dk_s, dv_s, w_out, w_in,
-    sem_sa, sem_ra, sem_sb, sem_rb, sem_tq, sem_kq, sem_tk, sem_kk,
+    sem_sa, sem_ra, sem_sb, sem_rb, sem_tq, sem_kq, sem_tk, sem_kk, sem_tv, sem_kv,
     sem_og, sem_up, sem_down, sem_sib, sem_ws, sem_wr, sem_in,
 ):
     rows, width = q_ref.shape
@@ -110,9 +110,23 @@
     set_a = (send_a, recv_a, sem_sa, sem_ra)
     set_b = (send_b, recv_b, sem_sb, sem_rb)
     set_q = (ret_q, back_q, sem_tq, sem_kq)
-    set_kv = (ret_kv, back_kv, sem_tk, sem_kk)
+    set_k = (ret_k, back_k, sem_tk, sem_kk)
+    set_v = (ret_v, back_v, sem_tv, sem_kv)
     can_up = z < line - 1
     can_down = z > 0
+
+    loads[0].wait()
+    pl.semaphore_wait(barrier, n - 1 + ndp - 1)
+
+    @pl.when(can_up)
+    def _():
+        relay(me, sem_up.at[z], me + 2).start()
+
+    @pl.when(can_down)
+    def _():
+        relay(me, sem_down.at[z], me - 2).start()
+
+    relay(me, sem_sib.at[z], sib).start()
 
     loads[1].wait()
     loads[2].wait()
@@ -130,20 +144,31 @@
                     [flip[which, base:base + span, :], jnp.zeros((BAND - span, rows), F32)], axis=0
                 )
             send_a[d, which * BAND:(which + 1) * BAND, :] = part.astype(BF16)
-    loads[0].wait()
-    pl.semaphore_wait(barrier, n - 1 + ndp - 1)
     send_all(*set_a)
-
-    @pl.when(can_up)
-    def _():
-        relay(me, sem_up.at[z], me + 2).start()
-
-    @pl.when(can_down)
-    def _():
-        relay(me, sem_down.at[z], me - 2).start()
-
-    relay(me, sem_sib.at[z], sib).start()
     recv_a[pl.ds(me, 1)] = send_a[pl.ds(me, 1)]
+    def relay_step(step):
+        @pl.when(z >= step)
+        def _():
+            src = me - 2 * step
+            relay(src, sem_up.at[z - step], sib).wait_recv()
+
+            @pl.when(can_up)
+            def _():
+                relay(src, sem_up.at[z - step], me + 2).start()
+
+            relay(src, sem_sib.at[z - step], sib).start()
+
+        @pl.when(z + step < line)
+        def _():
+            src = me + 2 * step
+            relay(src, sem_down.at[z + step], sib).wait_recv()
+
+            @pl.when(can_down)
+            def _():
+                relay(src, sem_down.at[z + step], me - 2).start()
+
+            relay(src, sem_sib.at[z + step], sib).start()
+
     if two:
         for which in range(3):
             for d in range(n):
@@ -151,31 +176,9 @@
                 send_b[d, which * 64:(which + 1) * 64, :] = flip[
                     which, base + BAND:base + span, :
                 ].astype(BF16)
+        relay_step(1)
         send_all(*set_b)
         recv_b[pl.ds(me, 1)] = send_b[pl.ds(me, 1)]
-
-    def relay_step(step):
-        @pl.when(z >= step)
-        def _():
-            src = me - 2 * step
-            relay(src, sem_up.at[z - step], sib).wait_recv()
-
-            @pl.when(can_up)
-            def _():
-                relay(src, sem_up.at[z - step], me + 2).start()
-
-            relay(src, sem_sib.at[z - step], sib).start()
-
-        @pl.when(z + step < line)
-        def _():
-            src = me + 2 * step
-            relay(src, sem_down.at[z + step], sib).wait_recv()
-
-            @pl.when(can_down)
-            def _():
-                relay(src, sem_down.at[z + step], me - 2).start()
-
-            relay(src, sem_sib.at[z + step], sib).start()
 
     ends = []
     total = jnp.int32(0)
@@ -273,12 +276,13 @@
 
     wait_all(*set_a)
     forward(0)
-    relay_step(1)
+    if not two:
+        relay_step(1)
+    if line > 2:
+        relay_step(2)
     if two:
         wait_all(*set_b)
         forward(1)
-    if line > 2:
-        relay_step(2)
     loads[4].wait()
     near = jnp.minimum(z, line - 1 - z)
     toward = jnp.where(z < line - 1 - z, 1, -1)
@@ -294,20 +298,20 @@
         relay(2 * chip + 1 - core, sem_sib.at[chip], sib).wait_recv()
         backward(chip)
 
-    tall = ret_q.shape[1]
-    for s in range(n):
-        lanes = slice(s * rows, (s + 1) * rows)
-        for which, (ref, factor) in enumerate(((dk_s, scale), (dv_s, None))):
+    for ref, into, whole, factor in ((dk_s, ret_k, set_k, scale), (dv_s, ret_v, set_v, None)):
+        for s in range(n):
+            lanes = slice(s * rows, (s + 1) * rows)
             if two:
                 part = jnp.concatenate([ref[0, 0:72, lanes], ref[1, 8:80, lanes]], axis=0)
             else:
                 part = ref[0, :, lanes]
             if factor is not None:
                 part = part * factor
-            ret_kv[s, which * tall:(which + 1) * tall, :] = part.astype(BF16)
-    send_all(*set_kv)
+            into[s] = part.astype(BF16)
+        send_all(*whole)
     back_q[pl.ds(me, 1)] = ret_q[pl.ds(me, 1)]
-    back_kv[pl.ds(me, 1)] = ret_kv[pl.ds(me, 1)]
+    back_k[pl.ds(me, 1)] = ret_k[pl.ds(me, 1)]
+    back_v[pl.ds(me, 1)] = ret_v[pl.ds(me, 1)]
 
     piece = width // ndp
     term = dot(att_t[0:span, :].astype(BF16), og_all[...].reshape(seq, width))
@@ -328,14 +332,14 @@
         reduce_copy(lax.rem(dp + p, ndp), dp).start()
     w_in[pl.ds(dp, 1)] = w_out[pl.ds(dp, 1)]
 
-    def unpack(ref, first, out):
+    def unpack(ref, out):
         for d in range(n):
-            flip[0, d * span:(d + 1) * span, :] = ref[d, first:first + tall, :].astype(F32)[0:span]
+            flip[0, d * span:(d + 1) * span, :] = ref[d].astype(F32)[0:span]
         for g in range(groups):
             out[:, g * rows:(g + 1) * rows] = flip[0, g * rows:(g + 1) * rows, :].T.astype(BF16)
 
     wait_all(*set_q)
-    unpack(back_q, 0, dq_ref)
+    unpack(back_q, dq_ref)
     for p in range(1, ndp):
         peer = lax.rem(dp + p, ndp)
         reduce_copy(peer, peer).wait_recv()
@@ -361,22 +365,26 @@
         def _():
             relay(2 * part + core, sem_down.at[part], sib).wait_send()
 
-    wait_all(*set_kv)
-    unpack(back_kv, 0, dk_ref)
-    unpack(back_kv, tall, dv_ref)
-    wait_sent(*set_kv)
+    wait_all(*set_k)
+    unpack(back_k, dk_ref)
+    wait_all(*set_v)
+    unpack(back_v, dv_ref)
+    wait_sent(*set_k)
+    wait_sent(*set_v)
 
 
 def finish(*refs):
-    count = len(refs) // 2
-    sems = refs[-1]
-    copies = [
-        pltpu.make_async_copy(refs[i], refs[count + i], sems.at[i]) for i in range(count)
-    ]
-    for copy in copies:
-        copy.start()
-    for copy in copies:
-        copy.wait()
+    count = len(refs) // 3
+    sources, results, held, sems = refs[:count], refs[count:2 * count], refs[2 * count:-1], refs[-1]
+    loads = [pltpu.make_async_copy(sources[i], held[i], sems.at[0, i]) for i in range(count)]
+    stores = [pltpu.make_async_copy(held[i], results[i], sems.at[1, i]) for i in range(count)]
+    for load in loads:
+        load.start()
+    for load, store in zip(loads, stores):
+        load.wait()
+        store.start()
+    for store in stores:
+        store.wait()
 
 
 def local(n, ndp, queries, keys, values, out_grad, out_weight, extents):
@@ -415,9 +423,11 @@
             buf((n, 3 * BAND, rows), BF16),
             buf((n, 3 * 64, rows), BF16),
             buf((n, padded, rows), BF16),
-            buf((n, 2 * padded, rows), BF16),
-            buf((n, padded, rows), BF16),
-            buf((n, 2 * padded, rows), BF16),
+            buf((n, padded, rows), BF16),
+            buf((n, padded, rows), BF16),
+            buf((n, padded, rows), BF16),
+            buf((n, padded, rows), BF16),
+            buf((n, padded, rows), BF16),
             buf((per, BAND, seq), BF16),
             buf((per, BAND, seq), BF16),
             buf((per, BAND, seq), BF16),
@@ -430,7 +440,7 @@
             buf((ndp, padded, width // ndp), BF16),
             buf((ndp, padded, width // ndp), BF16),
         ]
-        + [dma((n,))] * 8
+        + [dma((n,))] * 10
         + [dma((n,)), dma((line,)), dma((line,)), dma((line,)), dma((ndp,)), dma((ndp,)), dma((5,))],
         compiler_params=pltpu.CompilerParams(
             collective_id=0, has_side_effects=True, vmem_limit_bytes=56 * 2**20
@@ -445,7 +455,7 @@
         out_shape=(grad, grad, grad, weight),
         in_specs=[hbm] * 4,
         out_specs=(hbm, hbm, hbm, hbm),
-        scratch_shapes=[dma((4,))],
+        scratch_shapes=[buf(part.shape, part.dtype) for part in parts] + [dma((2, 4))],
         compiler_params=pltpu.CompilerParams(vmem_limit_bytes=56 * 2**20),
     )(*parts)
 

time: 102 us -> 72 us (0.71); the launches traced: 100 us -> 71.7 us
  Pallas kernels: 99.7 us -> 71 us
    pallas_call x1, Pallas kernels: 34.6 us -> 2.01 us  [local(): pl.pallas_call(finish, out_shape=(grad, grad, grad, weight), in_specs=[hb...]
    pallas_call x1, Pallas kernels: 65 us -> 69 us  [local(): pl.pallas_call(functools.partial(kernel, n, ndp, images), out_shape=(grad...]
where the time goes in v3:
time: 72 us; the launch traced here: 71.7 us
  Pallas kernels  71 us (99%)
    pallas_call x1, Pallas kernels, local(): pl.pallas_call(functools.partial(kernel, n, ndp, images), out_shape=(grad...  69 us
    pallas_call x1, Pallas kernels, local(): pl.pallas_call(finish, out_shape=(grad, grad, grad, weight), in_specs=[hb...  2.01 us

profile of v3, /device:TPU:0, one launch (start us, length us, event | category | flops | bytes accessed | tf_op | source)
XLA Modules:
  0.0 71.7 jit_solution(9482326051102839590)
XLA Ops:
  0.6 69.0 %shard_map.93 = (bf16[128,1152]{1,0:T(8,128)(2,1)}, bf16[128,1152]{1,0:T(8,128)(2,1)}, bf16[128,1152]{1,0:T(8,128)(2,1)}, f32[144,288]{1,0:T(8,128)}) custom-call(s32[1,8]{1,0:T(1,128)} %ext_ref.1, bf16[128,1152]{1,0:T(8,128)(2,1)} %q_hbm.1, bf16[128,1152]{1,0:T(8,128)(2,1)} %k_hbm.1, bf16[128,1152]{1,0:T(8,128)(2,1)} %v_hbm.1, bf16[128,1152]{1,0:T(8,128)(2,1)} %og_hbm.1, ...), custom_call_target="tpu_custom_call" | custom-call | flops 1509949440 | bytes 2949120 | tf_op jit(solution)/shard_map/pallas_call | solution.py:409
  69.7 2.0 %shard_map.94 = (bf16[128,1152]{1,0:T(8,128)(2,1)}, bf16[128,1152]{1,0:T(8,128)(2,1)}, bf16[128,1152]{1,0:T(8,128)(2,1)}, f32[144,288]{1,0:T(8,128)}) custom-call(bf16[128,1152]{1,0:T(8,128)(2,1)} %get-tuple-element.8.refs_0_, bf16[128,1152]{1,0:T(8,128)(2,1)} %get-tuple-element.9.refs_1_, bf16[128,1152]{1,0:T(8,128)(2,1)} %get-tuple-element.10.refs_2_, ...), custom_call_target="tpu_custom_call" | custom-call | tf_op jit(solution)/shard_map/pallas_call | solution.py:453

commit v4 on v3

--- a/solution.py
+++ b/solution.py
@@ -29,7 +29,7 @@
     dq_ref, dk_ref, dv_ref, dw_ref,
     q_ref, k_ref, v_ref, og_all, w_mine, flip, send_a, send_b, recv_a, recv_b,
     ret_q, ret_k, ret_v, back_q, back_k, back_v,
-    xq, xk, xv, kn, vn, probs_all, att_t, dk_s, dv_s, w_out, w_in,
+    xq, xk, xv, kn, vn, grown_all, inverse_all, att_t, dk_s, dv_s, w_out, w_in,
     sem_sa, sem_ra, sem_sb, sem_rb, sem_tq, sem_kq, sem_tk, sem_kk, sem_tv, sem_kv,
     sem_og, sem_up, sem_down, sem_sib, sem_ws, sem_wr, sem_in,
 ):
@@ -115,19 +115,6 @@
     can_up = z < line - 1
     can_down = z > 0
 
-    loads[0].wait()
-    pl.semaphore_wait(barrier, n - 1 + ndp - 1)
-
-    @pl.when(can_up)
-    def _():
-        relay(me, sem_up.at[z], me + 2).start()
-
-    @pl.when(can_down)
-    def _():
-        relay(me, sem_down.at[z], me - 2).start()
-
-    relay(me, sem_sib.at[z], sib).start()
-
     loads[1].wait()
     loads[2].wait()
     loads[3].wait()
@@ -144,7 +131,19 @@
                     [flip[which, base:base + span, :], jnp.zeros((BAND - span, rows), F32)], axis=0
                 )
             send_a[d, which * BAND:(which + 1) * BAND, :] = part.astype(BF16)
+    loads[0].wait()
+    pl.semaphore_wait(barrier, n - 1 + ndp - 1)
     send_all(*set_a)
+
+    @pl.when(can_up)
+    def _():
+        relay(me, sem_up.at[z], me + 2).start()
+
+    @pl.when(can_down)
+    def _():
+        relay(me, sem_down.at[z], me - 2).start()
+
+    relay(me, sem_sib.at[z], sib).start()
     recv_a[pl.ds(me, 1)] = send_a[pl.ds(me, 1)]
     def relay_step(step):
         @pl.when(z >= step)
@@ -176,7 +175,6 @@
                 send_b[d, which * 64:(which + 1) * 64, :] = flip[
                     which, base + BAND:base + span, :
                 ].astype(BF16)
-        relay_step(1)
         send_all(*set_b)
         recv_b[pl.ds(me, 1)] = send_b[pl.ds(me, 1)]
 
@@ -224,7 +222,7 @@
             xk[h, :, lanes] = ks.astype(BF16)
             xv[h, :, lanes] = vs.astype(BF16)
             kn[h, lanes, :] = ks.T.astype(BF16)
-            vn[h, lanes, :] = vs.T.astype(BF16)
+            vn[h, lanes, :] = jnp.where(own, take(2), 1.0).T.astype(BF16)
 
         dk_s[h] = jnp.zeros((BAND, seq), F32)
         dv_s[h] = jnp.zeros((BAND, seq), F32)
@@ -236,9 +234,10 @@
             top = jnp.max(scores, axis=0, keepdims=True)
             grown = jnp.exp2((scores - top) * turn)
             inverse = 1.0 / jnp.sum(grown, axis=0, keepdims=True)
-            probs = grown * inverse
-            probs_all[h, :, lanes] = probs
-            attended = dot(xv[h], probs.astype(BF16)).astype(BF16).astype(F32)
+            inverse_all[h, :, lanes] = inverse
+            low = grown.astype(BF16)
+            grown_all[h, :, lanes] = low
+            attended = (dot(xv[h], low) * inverse).astype(BF16).astype(F32)
             if h == 0:
                 att_t[0:BAND, lanes] = attended
             else:
@@ -254,16 +253,23 @@
         parts = []
         for h in range(per):
             off = 64 * h
-            back = jnp.where(owned(h, pair), backs[off:off + BAND], 0.0).astype(BF16)
-            delta = jnp.sum(
-                back.astype(F32) * att_t[off:off + BAND, lanes], axis=0, keepdims=True
-            )
-            probs = probs_all[h, :, lanes]
-            dprobs = dot(vn[h], back)
-            dscores = (probs * (dprobs - delta)).astype(BF16)
-            parts.append(dot(xk[h], dscores) * scale)
-            dk_s[h] += dot(xq[h, :, lanes], dscores, NT)
-            dv_s[h] += dot(back, probs.astype(BF16), NT)
+            extra = HEAD if h == 0 else 0
+            back = jnp.where(owned(h, pair), backs[off:off + BAND], 0.0).astype(BF16).astype(F32)
+            delta = jnp.sum(back * att_t[off:off + BAND, lanes], axis=0, keepdims=True)
+            high = delta.astype(BF16).astype(F32)
+            middle = (delta - high).astype(BF16).astype(F32)
+            row = lax.broadcasted_iota(jnp.int32, (BAND, pair), 0) - extra
+            full = jnp.where(
+                row == 0, -high,
+                jnp.where(row == 1, -middle, jnp.where(row == 2, high + middle - delta, back)),
+            ).astype(BF16)
+            inverse = inverse_all[h, :, lanes]
+            grown = grown_all[h, :, lanes]
+            dscores = (grown.astype(F32) * dot(vn[h], full)).astype(BF16)
+            parts.append(dot(xk[h], dscores) * (inverse * scale))
+            queries = (xq[h, :, lanes].astype(F32) * inverse).astype(BF16)
+            dk_s[h] += dot(queries, dscores, NT)
+            dv_s[h] += dot((back * inverse).astype(BF16), grown, NT)
         done = jnp.concatenate([parts[0][0:72], parts[1][8:80]], axis=0) if two else parts[0]
         for j in range(2):
             peer = 2 * chip + j
@@ -276,13 +282,12 @@
 
     wait_all(*set_a)
     forward(0)
-    if not two:
-        relay_step(1)
-    if line > 2:
-        relay_step(2)
+    relay_step(1)
     if two:
         wait_all(*set_b)
         forward(1)
+    if line > 2:
+        relay_step(2)
     loads[4].wait()
     near = jnp.minimum(z, line - 1 - z)
     toward = jnp.where(z < line - 1 - z, 1, -1)
@@ -433,7 +438,8 @@
             buf((per, BAND, seq), BF16),
             buf((per, seq, BAND), BF16),
             buf((per, seq, BAND), BF16),
-            buf((per, seq, seq), F32),
+            buf((per, seq, seq), BF16),
+            buf((per, 1, seq), F32),
             buf((padded, seq), F32),
             buf((per, BAND, seq), F32),
             buf((per, BAND, seq), F32),

time: 72 us -> 70.4 us (0.978)
  Pallas kernels: 71 us -> 69.5 us
    pallas_call x1, Pallas kernels: 69 us -> 67.5 us  [local(): pl.pallas_call(functools.partial(kernel, n, ndp, images), out_shape=(grad...]
where the time goes in v4:
time: 70.4 us; the launch traced here: 70.2 us
  Pallas kernels  69.5 us (99%)
    pallas_call x1, Pallas kernels, local(): pl.pallas_call(functools.partial(kernel, n, ndp, images), out_shape=(grad...  67.5 us
    pallas_call x1, Pallas kernels, local(): pl.pallas_call(finish, out_shape=(grad, grad, grad, weight), in_specs=[hb...  2.01 us

profile of v4, /device:TPU:0, one launch (start us, length us, event | category | flops | bytes accessed | tf_op | source)
XLA Modules:
  0.0 70.2 jit_solution(6026872086803013147)
XLA Ops:
  0.6 67.5 %shard_map.93 = (bf16[128,1152]{1,0:T(8,128)(2,1)}, bf16[128,1152]{1,0:T(8,128)(2,1)}, bf16[128,1152]{1,0:T(8,128)(2,1)}, f32[144,288]{1,0:T(8,128)}) custom-call(s32[1,8]{1,0:T(1,128)} %ext_ref.1, bf16[128,1152]{1,0:T(8,128)(2,1)} %q_hbm.1, bf16[128,1152]{1,0:T(8,128)(2,1)} %k_hbm.1, bf16[128,1152]{1,0:T(8,128)(2,1)} %v_hbm.1, bf16[128,1152]{1,0:T(8,128)(2,1)} %og_hbm.1, ...), custom_call_target="tpu_custom_call" | custom-call | flops 1509949440 | bytes 2949120 | tf_op jit(solution)/shard_map/pallas_call | solution.py:414
  68.2 2.0 %shard_map.94 = (bf16[128,1152]{1,0:T(8,128)(2,1)}, bf16[128,1152]{1,0:T(8,128)(2,1)}, bf16[128,1152]{1,0:T(8,128)(2,1)}, f32[144,288]{1,0:T(8,128)}) custom-call(bf16[128,1152]{1,0:T(8,128)(2,1)} %get-tuple-element.8.refs_0_, bf16[128,1152]{1,0:T(8,128)(2,1)} %get-tuple-element.9.refs_1_, bf16[128,1152]{1,0:T(8,128)(2,1)} %get-tuple-element.10.refs_2_, ...), custom_call_target="tpu_custom_call" | custom-call | tf_op jit(solution)/shard_map/pallas_call | solution.py:459

commit v5 on v4

--- a/solution.py
+++ b/solution.py
@@ -93,7 +93,8 @@
     def send_all(out, into, send_sem, recv_sem):
         @pl.loop(1, n)
         def _(p):
-            exchange(out, into, send_sem, recv_sem, lax.rem(me + p, n), me).start()
+            step = jnp.where(p <= n // 2, n // 2 + p - 1, p - n // 2)
+            exchange(out, into, send_sem, recv_sem, lax.rem(me + step, n), me).start()
 
     def wait_all(out, into, send_sem, recv_sem):
         @pl.loop(1, n)
@@ -283,11 +284,11 @@
     wait_all(*set_a)
     forward(0)
     relay_step(1)
+    if line > 2:
+        relay_step(2)
     if two:
         wait_all(*set_b)
         forward(1)
-    if line > 2:
-        relay_step(2)
     loads[4].wait()
     near = jnp.minimum(z, line - 1 - z)
     toward = jnp.where(z < line - 1 - z, 1, -1)

time: 70.4 us -> 73.9 us (1.050)
  Pallas kernels: 69.5 us -> 73.1 us
    pallas_call x1, Pallas kernels: 67.5 us -> 71.1 us  [local(): pl.pallas_call(functools.partial(kernel, n, ndp, images), out_shape=(grad...]
where the time goes in v5:
time: 73.9 us; the launch traced here: 73.7 us
  Pallas kernels  73.1 us (99%)
    pallas_call x1, Pallas kernels, local(): pl.pallas_call(functools.partial(kernel, n, ndp, images), out_shape=(grad...  71.1 us
    pallas_call x1, Pallas kernels, local(): pl.pallas_call(finish, out_shape=(grad, grad, grad, weight), in_specs=[hb...  2.01 us

profile of v5, /device:TPU:0, one launch (start us, length us, event | category | flops | bytes accessed | tf_op | source)
XLA Modules:
  0.0 73.7 jit_solution(8223213414571713094)
XLA Ops:
  0.6 71.1 %shard_map.93 = (bf16[128,1152]{1,0:T(8,128)(2,1)}, bf16[128,1152]{1,0:T(8,128)(2,1)}, bf16[128,1152]{1,0:T(8,128)(2,1)}, f32[144,288]{1,0:T(8,128)}) custom-call(s32[1,8]{1,0:T(1,128)} %ext_ref.1, bf16[128,1152]{1,0:T(8,128)(2,1)} %q_hbm.1, bf16[128,1152]{1,0:T(8,128)(2,1)} %k_hbm.1, bf16[128,1152]{1,0:T(8,128)(2,1)} %v_hbm.1, bf16[128,1152]{1,0:T(8,128)(2,1)} %og_hbm.1, ...), custom_call_target="tpu_custom_call" | custom-call | flops 1509949440 | bytes 2949120 | tf_op jit(solution)/shard_map/pallas_call | solution.py:415
  71.7 2.0 %shard_map.94 = (bf16[128,1152]{1,0:T(8,128)(2,1)}, bf16[128,1152]{1,0:T(8,128)(2,1)}, bf16[128,1152]{1,0:T(8,128)(2,1)}, f32[144,288]{1,0:T(8,128)}) custom-call(bf16[128,1152]{1,0:T(8,128)(2,1)} %get-tuple-element.8.refs_0_, bf16[128,1152]{1,0:T(8,128)(2,1)} %get-tuple-element.9.refs_1_, bf16[128,1152]{1,0:T(8,128)(2,1)} %get-tuple-element.10.refs_2_, ...), custom_call_target="tpu_custom_call" | custom-call | tf_op jit(solution)/shard_map/pallas_call | solution.py:460

commit v6 on v4

--- a/solution.py
+++ b/solution.py
@@ -286,15 +286,13 @@
     if two:
         wait_all(*set_b)
         forward(1)
-    if line > 2:
-        relay_step(2)
     loads[4].wait()
     near = jnp.minimum(z, line - 1 - z)
     toward = jnp.where(z < line - 1 - z, 1, -1)
 
     @pl.loop(0, line)
     def _(i):
-        @pl.when((i >= 2) & (i + 1 < line))
+        @pl.when((i >= 1) & (i + 1 < line))
         def _():
             relay_step(i + 1)
 

time: 70.4 us -> 70.3 us (level)
  no operation moved by 1% of the time
where the time goes in v6:
time: 70.3 us; the launch traced here: 70.1 us
  Pallas kernels  69.5 us (99%)
    pallas_call x1, Pallas kernels, local(): pl.pallas_call(functools.partial(kernel, n, ndp, images), out_shape=(grad...  67.5 us
    pallas_call x1, Pallas kernels, local(): pl.pallas_call(finish, out_shape=(grad, grad, grad, weight), in_specs=[hb...  2.01 us

profile of v6, /device:TPU:0, one launch (start us, length us, event | category | flops | bytes accessed | tf_op | source)
XLA Modules:
  0.0 70.1 jit_solution(58634415782726143)
XLA Ops:
  0.6 67.5 %shard_map.93 = (bf16[128,1152]{1,0:T(8,128)(2,1)}, bf16[128,1152]{1,0:T(8,128)(2,1)}, bf16[128,1152]{1,0:T(8,128)(2,1)}, f32[144,288]{1,0:T(8,128)}) custom-call(s32[1,8]{1,0:T(1,128)} %ext_ref.1, bf16[128,1152]{1,0:T(8,128)(2,1)} %q_hbm.1, bf16[128,1152]{1,0:T(8,128)(2,1)} %k_hbm.1, bf16[128,1152]{1,0:T(8,128)(2,1)} %v_hbm.1, bf16[128,1152]{1,0:T(8,128)(2,1)} %og_hbm.1, ...), custom_call_target="tpu_custom_call" | custom-call | flops 1509949440 | bytes 2949120 | tf_op jit(solution)/shard_map/pallas_call | solution.py:412
  68.1 2.0 %shard_map.94 = (bf16[128,1152]{1,0:T(8,128)(2,1)}, bf16[128,1152]{1,0:T(8,128)(2,1)}, bf16[128,1152]{1,0:T(8,128)(2,1)}, f32[144,288]{1,0:T(8,128)}) custom-call(bf16[128,1152]{1,0:T(8,128)(2,1)} %get-tuple-element.8.refs_0_, bf16[128,1152]{1,0:T(8,128)(2,1)} %get-tuple-element.9.refs_1_, bf16[128,1152]{1,0:T(8,128)(2,1)} %get-tuple-element.10.refs_2_, ...), custom_call_target="tpu_custom_call" | custom-call | tf_op jit(solution)/shard_map/pallas_call | solution.py:457
